TPU v7x, 512 devices: a whole 4x4x16 slice. The times are simulated.
512 devices in a mesh: dp: 8 (over z_lo), pipe: 4 (over x), seq: 16 (over z_hi, y, core).
Axes of the slice: x: 4, y: 4, z: 16 (z_hi: 2, z_lo: 8; z = z_hi * 8 + z_lo), core: 2. Of those that a mesh axis runs over, the one named last changes fastest.
Arguments:
- queries: bfloat16 [4, 8, 2048, 2048], P('pipe', 'dp', 'seq'), may hold values from -6 to 6
- keys: bfloat16 [4, 8, 2048, 512], P('pipe', 'dp', 'seq'), may hold values from -6 to 6
- values: bfloat16 [4, 8, 2048, 512], P('pipe', 'dp', 'seq'), may hold values from -6 to 6
- grad_next: bfloat16 [4, 8, 2048, 2048], P('pipe', 'dp', 'seq'), may hold values from -6 to 6
- normed: bfloat16 [4, 8, 2048, 4096], P('pipe', 'dp', 'seq'), may hold values from -6 to 6
- value_weight: bfloat16 [4, 4096, 512], P('pipe', 'seq'), may hold values from -0.09375 to 0.09375
Outputs:
- grad_queries: bfloat16 [4, 8, 2048, 2048], P('pipe', 'dp', 'seq')
- grad_keys: bfloat16 [4, 8, 2048, 512], P('pipe', 'dp', 'seq')
- grad_normed: bfloat16 [4, 8, 2048, 4096], P('pipe', 'dp', 'seq')
- grad_value_weight: float32 [4, 4096, 512], P('pipe', 'seq')
All inputs are finite; a program needn't handle non-finite values.
Results may differ from a plain program's by a relative error of at most 0.019.
Values may be sent and summed in bfloat16 or wider, within the bound.
A program may use at most 64 MiB of HBM per device.

v0:
```python
import jax
import jax.numpy as jnp
from jax import lax
from jax.sharding import PartitionSpec as P

HEAD = 128
HQ = 16
masked_value = -1e30


def passed_along(block, axis, distance):
    devices = range(lax.axis_size(axis))
    route = [((i - distance) % len(devices), i) for i in devices]
    return lax.ppermute(block, axis, route)


def attend(query_head, key_head, value_head, upstream_head):
    length = query_head.shape[0]
    block_rows = min(512, length)
    factor = HEAD ** (-0.5)
    query_parts = []
    grad_key = jnp.zeros((length, HEAD), jnp.float32)
    grad_value = jnp.zeros((length, HEAD), jnp.float32)
    for block_index in range(length // block_rows):
        first_row = block_index * block_rows
        finish = first_row + block_rows
        query_block = query_head[first_row:finish]
        upstream_block = upstream_head[first_row:finish]
        key_prefix = key_head[:finish]
        value_prefix = value_head[:finish]
        row_pos = first_row + jnp.arange(block_rows, dtype=jnp.int32)[:, None]
        col_pos = jnp.arange(finish, dtype=jnp.int32)[None, :]
        scores = jnp.where(
            col_pos <= row_pos,
            lax.dot_general(
                query_block,
                key_prefix,
                (((1,), (1,)), ((), ())),
                preferred_element_type=jnp.float32,
            )
            * factor,
            masked_value,
        )
        row_top = jnp.max(scores, axis=1, keepdims=True)
        row_total = jnp.sum(jnp.exp(scores - row_top), axis=1, keepdims=True)
        probs_half = (jnp.exp(scores - row_top) / row_total).astype(jnp.bfloat16)
        attn_out = jnp.dot(probs_half, value_prefix, preferred_element_type=jnp.float32)
        row_delta = jnp.sum(upstream_block.astype(jnp.float32) * attn_out, axis=1, keepdims=True)
        grad_probs = lax.dot_general(
            upstream_block,
            value_prefix,
            (((1,), (1,)), ((), ())),
            preferred_element_type=jnp.float32,
        )
        grad_scores = (jnp.exp(scores - row_top) / row_total * (grad_probs - row_delta)).astype(
            jnp.bfloat16
        )
        query_parts.append(
            jnp.dot(grad_scores, key_prefix, preferred_element_type=jnp.float32) * factor
        )
        key_part = (
            lax.dot_general(
                grad_scores,
                query_block,
                (((0,), (0,)), ((), ())),
                preferred_element_type=jnp.float32,
            )
            * factor
        )
        value_part = lax.dot_general(
            probs_half, upstream_block, (((0,), (0,)), ((), ())), preferred_element_type=jnp.float32
        )
        grad_key = grad_key.at[:finish].add(key_part)
        grad_value = grad_value.at[:finish].add(value_part)
    return (jnp.concatenate(query_parts, axis=0), grad_key, grad_value)


def local(queries, keys, values, grad_next, normed, value_weight):
    query_rows = queries[0, 0]
    key_rows = keys[0, 0]
    value_rows = values[0, 0]
    normed_rows = normed[0, 0]
    value_proj = value_weight[0]
    upstream = passed_along(grad_next[0, 0], "pipe", -1)
    tokens = query_rows.shape[0]
    kv_heads = key_rows.shape[1] // HEAD
    repeats = HQ // kv_heads

    def widen(source):
        spread = jnp.broadcast_to(
            source.reshape(tokens, kv_heads, 1, HEAD), (tokens, kv_heads, repeats, HEAD)
        )
        return spread.reshape(tokens, kv_heads * repeats * HEAD)

    query_cols, key_cols, value_cols, upstream_cols = (
        lax.all_to_all(query_rows, "seq", split_axis=1, concat_axis=0, tiled=True),
        lax.all_to_all(widen(key_rows), "seq", split_axis=1, concat_axis=0, tiled=True),
        lax.all_to_all(widen(value_rows), "seq", split_axis=1, concat_axis=0, tiled=True),
        lax.all_to_all(upstream, "seq", split_axis=1, concat_axis=0, tiled=True),
    )
    head_grads = [attend(query_cols, key_cols, value_cols, upstream_cols)]
    query_terms = jnp.concatenate([entry[0] for entry in head_grads], axis=1).astype(jnp.bfloat16)
    key_terms = jnp.concatenate([entry[1] for entry in head_grads], axis=1).astype(jnp.bfloat16)
    value_terms = jnp.concatenate([entry[2] for entry in head_grads], axis=1).astype(jnp.bfloat16)
    back_query, back_key, back_value = (
        lax.all_to_all(query_terms, "seq", split_axis=0, concat_axis=1, tiled=True),
        lax.all_to_all(key_terms, "seq", split_axis=0, concat_axis=1, tiled=True),
        lax.all_to_all(value_terms, "seq", split_axis=0, concat_axis=1, tiled=True),
    )

    def grouped(head_terms):
        summed = head_terms.astype(jnp.float32).reshape(tokens, kv_heads, repeats, HEAD).sum(axis=2)
        return summed.reshape(tokens, kv_heads * HEAD).astype(jnp.bfloat16)

    key_grad_rows = grouped(back_key)
    value_grad_rows = grouped(back_value)
    normed_cols = lax.all_to_all(normed_rows, "seq", split_axis=1, concat_axis=0, tiled=True)
    all_value_grads = lax.all_gather(value_grad_rows, "seq", axis=0, tiled=True)
    weight_term = lax.dot_general(
        normed_cols, all_value_grads, (((0,), (0,)), ((), ())), preferred_element_type=jnp.float32
    )
    weight_grad = lax.psum(weight_term.astype(jnp.bfloat16), "dp").astype(jnp.float32)
    full_rows = lax.dot_general(
        value_grad_rows,
        lax.all_gather(value_proj, "seq", axis=0, tiled=True),
        (((1,), (1,)), ((), ())),
        preferred_element_type=jnp.float32,
    )
    input_grad = full_rows.astype(jnp.bfloat16)
    return (
        back_query[None, None],
        key_grad_rows[None, None],
        input_grad[None, None],
        weight_grad[None],
    )


def solution(mesh):
    placed = (
        P("pipe", "dp", "seq", None),
        P("pipe", "dp", "seq", None),
        P("pipe", "dp", "seq", None),
        P("pipe", "dp", "seq", None),
        P("pipe", "dp", "seq", None),
        P("pipe", "seq", None),
    )
    return jax.shard_map(
        local,
        mesh=mesh,
        in_specs=placed,
        out_specs=(
            P("pipe", "dp", "seq", None),
            P("pipe", "dp", "seq", None),
            P("pipe", "dp", "seq", None),
            P("pipe", "seq", None),
        ),
        check_vma=False,
    )
```

profile of v0, /device:TPU:2, one launch (start us, length us, event | category | flops | bytes accessed | tf_op | source)
XLA Modules:
  0.0 549.3 jit_solution(11475916848880484211)
XLA Ops:
  9.1 17.8 %all-to-all-start.1 = ((bf16[128,16,128]{2,0,1:T(8,128)(2,1)}), bf16[128,16,128]{2,0,1:T(8,128)(2,1)S(1)}, u32[]{:S(2)}, u32[]{:S(2)}) async-start(bf16[128,16,128]{2,0,1:T(8,128)(2,1)} %bitcast.3), calls=%async_computation.1 | async-start | bytes 1048576 | tf_op jit(solution)/shard_map/all_to_all | solution.py:97
  28.0 19.1 %all-to-all-done.1 = bf16[128,16,128]{2,0,1:T(8,128)(2,1)S(1)} async-done(((bf16[128,16,128]{2,0,1:T(8,128)(2,1)}), bf16[128,16,128]{2,0,1:T(8,128)(2,1)S(1)}, u32[]{:S(2)}, u32[]{:S(2)}) %all-to-all-start.1) | async-done | bytes 524320 | tf_op jit(solution)/shard_map/all_to_all | solution.py:97
  47.0 3.6 all-to-all-start
  50.6 2.4 collective-permute-start
  53.1 13.5 %collective-permute-done = bf16[128,2048]{1,0:T(8,128)(2,1)S(1)} collective-permute-done((bf16[128,2048]{1,0:T(8,128)(2,1)S(1)}, bf16[128,2048]{1,0:T(8,128)(2,1)S(1)}, u32[]{:S(2)}, u32[]{:S(2)}) %collective-permute-start) | collective-permute-done | bytes 524320 | tf_op jit(solution)/shard_map/ppermute | solution.py:14
  67.7 2.4 all-to-all-done
  70.1 11.9 %all-to-all-start.2 = ((bf16[128,16,128]{0,2,1:T(8,128)(2,1)}), bf16[128,16,128]{0,2,1:T(8,128)(2,1)}, u32[]{:S(2)}, u32[]{:S(2)}) async-start(bf16[128,16,128]{0,2,1:T(8,128)(2,1)} %bitcast.7), calls=%async_computation.2 | async-start | bytes 1048576 | tf_op jit(solution)/shard_map/all_to_all | solution.py:99
  89.1 2.7 fusion.2
  91.8 9.9 %all-to-all-done.2 = bf16[128,16,128]{0,2,1:T(8,128)(2,1)} async-done(((bf16[128,16,128]{0,2,1:T(8,128)(2,1)}), bf16[128,16,128]{0,2,1:T(8,128)(2,1)}, u32[]{:S(2)}, u32[]{:S(2)}) %all-to-all-start.2) | async-done | bytes 524320 | tf_op jit(solution)/shard_map/all_to_all | solution.py:99
  108.3 25.2 %all_to_all.128 = bf16[16,128,128]{2,1,0:T(8,128)(2,1)S(1)} all-to-all(bf16[16,128,128]{2,1,0:T(8,128)(2,1)S(1)} %bitcast.130), channel_id=1, replica_groups=mesh['dp'=8,'pipe'=4,'seq'=16] {'seq'}, dimensions={0} | all-to-all | bytes 1048576 | tf_op jit(solution)/shard_map/all_to_all | solution.py:108
  139.3 5.5 all-to-all-start.3
  144.7 2.3 copy.66
  147.0 17.4 %all-to-all-done.3 = bf16[128,16,128]{2,0,1:T(8,128)(2,1)} async-done(((bf16[128,16,128]{2,0,1:T(8,128)(2,1)}), bf16[128,16,128]{2,0,1:T(8,128)(2,1)}, u32[]{:S(2)}, u32[]{:S(2)}) %all-to-all-start.3) | async-done | bytes 524320 | tf_op jit(solution)/shard_map/all_to_all | solution.py:98
  164.4 5.3 all-to-all-start.7
  185.7 2.0 multiply_convert_fusion
  190.6 7.4 %all-to-all-done.7 = bf16[128,16,256]{0,2,1:T(8,128)(2,1)} async-done(((bf16[128,16,256]{0,2,1:T(8,128)(2,1)}), bf16[128,16,256]{0,2,1:T(8,128)(2,1)}, u32[]{:S(2)}, u32[]{:S(2)}) %all-to-all-start.7) | async-done | bytes 1048608 | tf_op jit(solution)/shard_map/all_to_all | solution.py:117
  198.1 10.7 %all-to-all-start.5 = ((bf16[16,128,128]{2,1,0:T(8,128)(2,1)}), bf16[16,128,128]{2,1,0:T(8,128)(2,1)}, u32[]{:S(2)}, u32[]{:S(2)}) async-start(bf16[16,128,128]{2,1,0:T(8,128)(2,1)} %bitcast.134), calls=%async_computation.5 | async-start | bytes 1048576 | tf_op jit(solution)/shard_map/all_to_all | solution.py:107
  213.8 42.3 %all-to-all-done.5 = bf16[16,128,128]{2,1,0:T(8,128)(2,1)} async-done(((bf16[16,128,128]{2,1,0:T(8,128)(2,1)}), bf16[16,128,128]{2,1,0:T(8,128)(2,1)}, u32[]{:S(2)}, u32[]{:S(2)}) %all-to-all-start.5) | async-done | bytes 524320 | tf_op jit(solution)/shard_map/all_to_all | solution.py:107
  256.1 9.1 %all-to-all-start.4 = ((bf16[16,128,128]{2,1,0:T(8,128)(2,1)}), bf16[16,128,128]{2,1,0:T(8,128)(2,1)S(1)}, u32[]{:S(2)}, u32[]{:S(2)}) async-start(bf16[16,128,128]{2,1,0:T(8,128)(2,1)} %bitcast.22), calls=%async_computation.4 | async-start | bytes 1048576 | tf_op jit(solution)/shard_map/all_to_all | solution.py:106
  268.8 25.7 %all-to-all-done.4 = bf16[16,128,128]{2,1,0:T(8,128)(2,1)S(1)} async-done(((bf16[16,128,128]{2,1,0:T(8,128)(2,1)}), bf16[16,128,128]{2,1,0:T(8,128)(2,1)S(1)}, u32[]{:S(2)}, u32[]{:S(2)}) %all-to-all-start.4) | async-done | bytes 524320 | tf_op jit(solution)/shard_map/all_to_all | solution.py:106
  295.9 3.0 fusion.23
  298.9 122.1 %all-gather.6.cloned.1.call-done = bf16[1,4096,512]{2,1,0:T(8,128)(2,1)} async-done(((bf16[1,256,512]{2,1,0:T(8,128)(2,1)}), bf16[1,4096,512]{2,1,0:T(8,128)(2,1)}) %all-gather.6.cloned.1.call-update) | async-done | bytes 4194320 | tf_op jit(solution)/shard_map/all_gather | solution.py:125
  421.0 4.7 fusion
  425.7 115.2 %all-reduce.4.cloned.1.call-done = bf16[1,256,512]{1,2,0:T(8,128)(2,1)} async-done(((bf16[1,256,512]{1,2,0:T(8,128)(2,1)}), bf16[1,256,512]{1,2,0:T(8,128)(2,1)}) %all-reduce.4.cloned.1.call-update) | async-done | bytes 262160 | tf_op jit(solution)/shard_map/psum | solution.py:122
  (139 shorter events, 53.8 us)
Async XLA Ops:
  7.2 19.8 %copy-start.25 = (bf16[1,1,128,2048]{3,2,1,0:T(8,128)(2,1)S(1)}, bf16[1,1,128,2048]{3,2,1,0:T(8,128)(2,1)}, u32[]{:S(2)}) copy-start(bf16[1,1,128,2048]{3,2,1,0:T(8,128)(2,1)} %param.26) | copy-start | bytes 1572868
  8.2 42.4 %copy-start.33 = (bf16[1,1,128,2048]{3,2,1,0:T(8,128)(2,1)S(1)}, bf16[1,1,128,2048]{3,2,1,0:T(8,128)(2,1)}, u32[]{:S(2)}) copy-start(bf16[1,1,128,2048]{3,2,1,0:T(8,128)(2,1)} %param.29) | copy-start | bytes 1572868
  9.1 37.9 %all-to-all-start.1 = ((bf16[128,16,128]{2,0,1:T(8,128)(2,1)}), bf16[128,16,128]{2,0,1:T(8,128)(2,1)S(1)}, u32[]{:S(2)}, u32[]{:S(2)}) async-start(bf16[128,16,128]{2,0,1:T(8,128)(2,1)} %bitcast.3), calls=%async_computation.1 | async-start | bytes 1048576 | tf_op jit(solution)/shard_map/all_to_all | solution.py:97
  47.0 38.5 %copy-start.10 = (bf16[128,16,128]{2,0,1:T(8,128)(2,1)}, bf16[128,16,128]{2,0,1:T(8,128)(2,1)S(1)}, u32[]{:S(2)}) copy-start(bf16[128,16,128]{2,0,1:T(8,128)(2,1)S(1)} %all-to-all-done.1) | copy-start | bytes 1572868
  47.0 23.1 %all-to-all-start = ((bf16[128,16,128]{0,2,1:T(8,128)(2,1)}), bf16[128,16,128]{0,2,1:T(8,128)(2,1)S(1)}, u32[]{:S(2)}, u32[]{:S(2)}) async-start(bf16[128,16,128]{0,2,1:T(8,128)(2,1)} %bitcast), calls=%async_computation | async-start | bytes 1048576 | tf_op jit(solution)/shard_map/all_to_all | solution.py:96
  50.6 16.0 %collective-permute-start = (bf16[128,2048]{1,0:T(8,128)(2,1)S(1)}, bf16[128,2048]{1,0:T(8,128)(2,1)S(1)}, u32[]{:S(2)}, u32[]{:S(2)}) collective-permute-start(bf16[128,2048]{1,0:T(8,128)(2,1)S(1)} %bitcast.157), channel_id=1, source_target_pairs={{16,0},{32,16},{48,32},{0,48},{17,1},{33,17},{49,33},{1,49},{18,2}... | collective-permute-start | bytes 1572872 | tf_op jit(solution)/shard_map/ppermute | solution.py:14
  67.6 15.1 %copy-start.26 = (bf16[4,128,128]{2,1,0:T(8,128)(2,1)}, bf16[4,128,128]{2,1,0:T(8,128)(2,1)S(1)}, u32[]{:S(2)}) copy-start(bf16[4,128,128]{2,1,0:T(8,128)(2,1)S(1)} %slice.253) | copy-start | bytes 393220
  67.7 15.4 %copy-start.20 = (bf16[8,128,128]{2,1,0:T(8,128)(2,1)}, bf16[8,128,128]{2,1,0:T(8,128)(2,1)S(1)}, u32[]{:S(2)}) copy-start(bf16[8,128,128]{2,1,0:T(8,128)(2,1)S(1)} %slice.257) | copy-start | bytes 786436
  67.7 16.5 %copy-start.17 = (bf16[12,128,128]{2,1,0:T(8,128)(2,1)}, bf16[12,128,128]{2,1,0:T(8,128)(2,1)S(1)}, u32[]{:S(2)}) copy-start(bf16[12,128,128]{2,1,0:T(8,128)(2,1)S(1)} %slice.261) | copy-start | bytes 1179652
  70.1 31.5 %all-to-all-start.2 = ((bf16[128,16,128]{0,2,1:T(8,128)(2,1)}), bf16[128,16,128]{0,2,1:T(8,128)(2,1)}, u32[]{:S(2)}, u32[]{:S(2)}) async-start(bf16[128,16,128]{0,2,1:T(8,128)(2,1)} %bitcast.7), calls=%async_computation.2 | async-start | bytes 1048576 | tf_op jit(solution)/shard_map/all_to_all | solution.py:99
  82.0 213.8 %all-gather.4.cloned.1.call-start = ((), (), s32[]{:S(2)}) async-start(), calls=%async_computation.8 | async-start | bytes 2228224 | tf_op jit(solution)/shard_map/all_gather | solution.py:118
  139.3 25.1 %all-to-all-start.3 = ((bf16[128,16,128]{2,0,1:T(8,128)(2,1)}), bf16[128,16,128]{2,0,1:T(8,128)(2,1)}, u32[]{:S(2)}, u32[]{:S(2)}) async-start(bf16[128,16,128]{2,0,1:T(8,128)(2,1)} %bitcast.131), calls=%async_computation.3 | async-start | bytes 1048576 | tf_op jit(solution)/shard_map/all_to_all | solution.py:98
  164.4 33.7 %all-to-all-start.7 = ((bf16[128,16,256]{0,2,1:T(8,128)(2,1)}), bf16[128,16,256]{0,2,1:T(8,128)(2,1)}, u32[]{:S(2)}, u32[]{:S(2)}) async-start(bf16[128,16,256]{0,2,1:T(8,128)(2,1)} %bitcast.122), calls=%async_computation.7 | async-start | bytes 2097152 | tf_op jit(solution)/shard_map/all_to_all | solution.py:117
  169.6 251.4 %all-gather.6.cloned.1.call-start = ((), (), s32[]{:S(2)}) async-start(), calls=%async_computation.10 | async-start | bytes 4456448 | tf_op jit(solution)/shard_map/all_gather | solution.py:125
  170.4 4.4 copy-start.7
  170.4 4.4 copy-start.28
  189.1 19.7 %copy-start.13 = (bf16[512,512]{0,1:T(8,128)(2,1)S(1)}, bf16[512,512]{0,1:T(8,128)(2,1)}, u32[]{:S(2)}) copy-start(bf16[512,512]{0,1:T(8,128)(2,1)} %copy-done.12) | copy-start | bytes 1572868
  189.1 21.1 %copy-start.9 = (bf16[512,1024]{1,0:T(8,128)(2,1)S(1)}, bf16[512,1024]{1,0:T(8,128)(2,1)}, u32[]{:S(2)}) copy-start(bf16[512,1024]{1,0:T(8,128)(2,1)} %copy-done.8) | copy-start | bytes 3145732
  190.6 21.0 %copy-start.3 = (bf16[512,1536]{1,0:T(8,128)(2,1)S(1)}, bf16[512,1536]{1,0:T(8,128)(2,1)}, u32[]{:S(2)}) copy-start(bf16[512,1536]{1,0:T(8,128)(2,1)} %copy-done.2) | copy-start | bytes 4718596
  190.6 21.0 %copy-start.18 = (bf16[12,128,128]{2,1,0:T(8,128)(2,1)S(1)}, bf16[12,128,128]{2,1,0:T(8,128)(2,1)}, u32[]{:S(2)}) copy-start(bf16[12,128,128]{2,1,0:T(8,128)(2,1)} %copy-done.17) | copy-start | bytes 1179652
  198.1 58.0 %all-to-all-start.5 = ((bf16[16,128,128]{2,1,0:T(8,128)(2,1)}), bf16[16,128,128]{2,1,0:T(8,128)(2,1)}, u32[]{:S(2)}, u32[]{:S(2)}) async-start(bf16[16,128,128]{2,1,0:T(8,128)(2,1)} %bitcast.134), calls=%async_computation.5 | async-start | bytes 1048576 | tf_op jit(solution)/shard_map/all_to_all | solution.py:107
  256.1 38.4 %all-to-all-start.4 = ((bf16[16,128,128]{2,1,0:T(8,128)(2,1)}), bf16[16,128,128]{2,1,0:T(8,128)(2,1)S(1)}, u32[]{:S(2)}, u32[]{:S(2)}) async-start(bf16[16,128,128]{2,1,0:T(8,128)(2,1)} %bitcast.22), calls=%async_computation.4 | async-start | bytes 1048576 | tf_op jit(solution)/shard_map/all_to_all | solution.py:106
  265.2 275.7 %all-reduce.4.cloned.1.call-start = ((), (), s32[]{:S(2)}) async-start(), calls=%async_computation.9 | async-start | bytes 524288 | tf_op jit(solution)/shard_map/psum | solution.py:122
  295.9 125.2 %copy-start.19 = (bf16[128,4,128]{0,2,1:T(8,128)(2,1)S(1)}, bf16[128,4,128]{0,2,1:T(8,128)(2,1)}, u32[]{:S(2)}) copy-start(bf16[128,4,128]{0,2,1:T(8,128)(2,1)} %copy.65) | copy-start | bytes 393220
  (21 other events, 42.3 us)
Sparse Core Ops, SparseCore 0:
  136.0 132.1 all-gather.3
  271.5 149.5 all-gather.5
  424.5 116.3 all-reduce.3
where the time goes:
time: 551 us; the launch traced here: 549 us
  waiting for transfers between devices  376 us (68%)
  starting transfers between devices  66.5 us (12%)
  matrix products  29.5 us (5%)
  local copies, waits for them, and re-layouts  29.1 us (5%)
  blocking collectives  25.2 us (5%)
  between operations  14.4 us (3%)
  other arithmetic  9.02 us (2%)
    all_gather x1, waiting for transfers between devices, local(): lax.all_gather(value_proj, 'seq', axis=0, tiled=True)  122 us
    psum x1, waiting for transfers between devices, local(): lax.psum(weight_term.astype(jnp.bfloat16), 'dp').astype(jnp.float32)  115 us
    all_to_all x1, waiting for transfers between devices, local(): lax.all_to_all(key_terms, 'seq', split_axis=0, concat_axis=1, tiled=True)  42.3 us
    all_to_all x1, waiting for transfers between devices, local(): lax.all_to_all(query_terms, 'seq', split_axis=0, concat_axis=1, tiled=True)  25.7 us
    all_to_all x1, blocking collectives, local(): lax.all_to_all(value_terms, 'seq', split_axis=0, concat_axis=1, tiled=True)  25.2 us
    all_to_all x1, waiting for transfers between devices, local(): lax.all_to_all(widen(key_rows), 'seq', split_axis=1, concat_axis=0, tiled...  19.1 us
    all_to_all x1, starting transfers between devices, local(): lax.all_to_all(widen(key_rows), 'seq', split_axis=1, concat_axis=0, tiled...  17.8 us
    all_to_all x1, waiting for transfers between devices, local(): lax.all_to_all(widen(value_rows), 'seq', split_axis=1, concat_axis=0, til...  17.4 us
  transfers between devices with their start and end apart: 11, of which 10 were waited for; matrix products, arithmetic and copies ran while one was open for 9% of the time, Pallas kernels for 0%

commit v1 on v0

--- a/solution.py
+++ b/solution.py
@@ -6,6 +6,13 @@
 HEAD = 128
 HQ = 16
 masked_value = -1e30
+
+
+def gather_over(x, axis, along):
+    devices = lax.axis_size(axis)
+    blocks = jnp.stack([x for _ in range(devices)])
+    blocks = lax.all_to_all(blocks, axis, split_axis=0, concat_axis=0)
+    return jnp.concatenate(blocks, axis=along)
 
 
 def passed_along(block, axis, distance):
@@ -122,7 +129,7 @@
     weight_grad = lax.psum(weight_term.astype(jnp.bfloat16), "dp").astype(jnp.float32)
     full_rows = lax.dot_general(
         value_grad_rows,
-        lax.all_gather(value_proj, "seq", axis=0, tiled=True),
+        gather_over(value_proj, "seq", 0),
         (((1,), (1,)), ((), ())),
         preferred_element_type=jnp.float32,
     )

time: 551 us -> 647 us (1.17)
  waiting for transfers between devices: 376 us -> 462 us
    all_gather x1, waiting for transfers between devices: 0.01 us -> 228 us  [local(): all_value_grads = lax.all_gather(value_grad_rows, 'seq', axis=0, tiled=True)]
    all_gather x1 -> x0, waiting for transfers between devices: 122 us -> none  [local(): lax.all_gather(value_proj, 'seq', axis=0, tiled=True)]
    ppermute x1, waiting for transfers between devices: 13.5 us -> 0.01 us  [passed_along(): return lax.ppermute(block, axis, route)]
    all_to_all x1, waiting for transfers between devices: 2.41 us -> 15.7 us  [local(): lax.all_to_all(query_rows, 'seq', split_axis=1, concat_axis=0, tiled=True)]
    all_to_all x1, waiting for transfers between devices: 42.3 us -> 30.3 us  [local(): lax.all_to_all(key_terms, 'seq', split_axis=0, concat_axis=1, tiled=True)]
    all_to_all x1, waiting for transfers between devices: 25.7 us -> 14 us  [local(): lax.all_to_all(query_terms, 'seq', split_axis=0, concat_axis=1, tiled=True)]
    psum x1, waiting for transfers between devices: 115 us -> 126 us  [local(): lax.psum(weight_term.astype(jnp.bfloat16), 'dp').astype(jnp.float32)]
    all_to_all x0 -> x1, starting transfers between devices: none -> 6.86 us  [gather_over(): blocks = lax.all_to_all(blocks, axis, split_axis=0, concat_axis=0)]
  transfers between devices with their start and end apart: 11 -> 11, of which waited for: 10 -> 9; matrix products, arithmetic and copies ran while one was open for 9% -> 8% of each run, Pallas kernels for 0% -> 0%
where the time goes in v1:
time: 647 us; the launch traced here: 646 us
  waiting for transfers between devices  462 us (71%)
  starting transfers between devices  71.2 us (11%)
  matrix products  31.2 us (5%)
  local copies, waits for them, and re-layouts  29 us (4%)
  blocking collectives  28 us (4%)
  between operations  14.8 us (2%)
  other arithmetic  9.06 us (1%)
    all_gather x1, waiting for transfers between devices, local(): all_value_grads = lax.all_gather(value_grad_rows, 'seq', axis=0, tiled=True)  228 us
    psum x1, waiting for transfers between devices, local(): lax.psum(weight_term.astype(jnp.bfloat16), 'dp').astype(jnp.float32)  126 us
    all_to_all x1, waiting for transfers between devices, local(): lax.all_to_all(key_terms, 'seq', split_axis=0, concat_axis=1, tiled=True)  30.3 us
    all_to_all x1, blocking collectives, local(): lax.all_to_all(value_terms, 'seq', split_axis=0, concat_axis=1, tiled=True)  28 us
    all_to_all x1, waiting for transfers between devices, local(): lax.all_to_all(widen(key_rows), 'seq', split_axis=1, concat_axis=0, tiled...  19.1 us
    all_to_all x1, starting transfers between devices, local(): lax.all_to_all(widen(key_rows), 'seq', split_axis=1, concat_axis=0, tiled...  17.8 us
    all_to_all x1, waiting for transfers between devices, local(): lax.all_to_all(query_rows, 'seq', split_axis=1, concat_axis=0, tiled=True)  15.7 us
    unnamed x105, local copies, waits for them, and re-layouts  15.7 us
  transfers between devices with their start and end apart: 11, of which 9 were waited for; matrix products, arithmetic and copies ran while one was open for 8% of the time, Pallas kernels for 0%

profile of v1, /device:TPU:2, one launch (start us, length us, event | category | flops | bytes accessed | tf_op | source)
XLA Modules:
  0.0 645.7 jit_solution(16145066822440414286)
XLA Ops:
  9.1 17.8 %all-to-all-start.1 = ((bf16[128,16,128]{2,0,1:T(8,128)(2,1)}), bf16[128,16,128]{2,0,1:T(8,128)(2,1)S(1)}, u32[]{:S(2)}, u32[]{:S(2)}) async-start(bf16[128,16,128]{2,0,1:T(8,128)(2,1)} %bitcast.3), calls=%async_computation.1 | async-start | bytes 1048576 | tf_op jit(solution)/shard_map/all_to_all | solution.py:104
  28.0 19.1 %all-to-all-done.1 = bf16[128,16,128]{2,0,1:T(8,128)(2,1)S(1)} async-done(((bf16[128,16,128]{2,0,1:T(8,128)(2,1)}), bf16[128,16,128]{2,0,1:T(8,128)(2,1)S(1)}, u32[]{:S(2)}, u32[]{:S(2)}) %all-to-all-start.1) | async-done | bytes 524320 | tf_op jit(solution)/shard_map/all_to_all | solution.py:104
  47.0 3.6 all-to-all-start
  50.6 2.4 collective-permute-start
  54.5 15.7 %all-to-all-done = bf16[128,16,128]{0,2,1:T(8,128)(2,1)S(1)} async-done(((bf16[128,16,128]{0,2,1:T(8,128)(2,1)}), bf16[128,16,128]{0,2,1:T(8,128)(2,1)S(1)}, u32[]{:S(2)}, u32[]{:S(2)}) %all-to-all-start) | async-done | bytes 524320 | tf_op jit(solution)/shard_map/all_to_all | solution.py:103
  71.0 7.6 %all-to-all-start.3 = ((bf16[128,16,128]{2,0,1:T(8,128)(2,1)}), bf16[128,16,128]{2,0,1:T(8,128)(2,1)S(1)}, u32[]{:S(2)}, u32[]{:S(2)}) async-start(bf16[128,16,128]{2,0,1:T(8,128)(2,1)} %bitcast.9), calls=%async_computation.3 | async-start | bytes 1048576 | tf_op jit(solution)/shard_map/all_to_all | solution.py:105
  84.7 2.8 fusion.60
  87.5 10.7 %all-to-all-done.3 = bf16[128,16,128]{2,0,1:T(8,128)(2,1)S(1)} async-done(((bf16[128,16,128]{2,0,1:T(8,128)(2,1)}), bf16[128,16,128]{2,0,1:T(8,128)(2,1)S(1)}, u32[]{:S(2)}, u32[]{:S(2)}) %all-to-all-start.3) | async-done | bytes 524320 | tf_op jit(solution)/shard_map/all_to_all | solution.py:105
  98.2 9.3 %all-to-all-start.2 = ((bf16[128,16,128]{0,2,1:T(8,128)(2,1)}), bf16[128,16,128]{0,2,1:T(8,128)(2,1)}, u32[]{:S(2)}, u32[]{:S(2)}) async-start(bf16[128,16,128]{0,2,1:T(8,128)(2,1)} %bitcast.7), calls=%async_computation.2 | async-start | bytes 1048576 | tf_op jit(solution)/shard_map/all_to_all | solution.py:106
  112.7 2.7 fusion.1
  115.4 11.8 %all-to-all-done.2 = bf16[128,16,128]{0,2,1:T(8,128)(2,1)} async-done(((bf16[128,16,128]{0,2,1:T(8,128)(2,1)}), bf16[128,16,128]{0,2,1:T(8,128)(2,1)}, u32[]{:S(2)}, u32[]{:S(2)}) %all-to-all-start.2) | async-done | bytes 524320 | tf_op jit(solution)/shard_map/all_to_all | solution.py:106
  127.2 6.2 all-to-all-start.8
  151.4 7.3 %all-to-all-done.8 = bf16[128,16,256]{0,2,1:T(8,128)(2,1)} async-done(((bf16[128,16,256]{0,2,1:T(8,128)(2,1)}), bf16[128,16,256]{0,2,1:T(8,128)(2,1)}, u32[]{:S(2)}, u32[]{:S(2)}) %all-to-all-start.8) | async-done | bytes 1048608 | tf_op jit(solution)/shard_map/all_to_all | solution.py:124
  158.7 9.9 %all-to-all-start.5 = ((bf16[16,128,128]{2,1,0:T(8,128)(2,1)}), bf16[16,128,128]{2,1,0:T(8,128)(2,1)}, u32[]{:S(2)}, u32[]{:S(2)}) async-start(bf16[16,128,128]{2,1,0:T(8,128)(2,1)} %bitcast.138), calls=%async_computation.5 | async-start | bytes 1048576 | tf_op jit(solution)/shard_map/all_to_all | solution.py:114
  174.1 30.3 %all-to-all-done.5 = bf16[16,128,128]{2,1,0:T(8,128)(2,1)} async-done(((bf16[16,128,128]{2,1,0:T(8,128)(2,1)}), bf16[16,128,128]{2,1,0:T(8,128)(2,1)}, u32[]{:S(2)}, u32[]{:S(2)}) %all-to-all-start.5) | async-done | bytes 524320 | tf_op jit(solution)/shard_map/all_to_all | solution.py:114
  204.3 7.2 %all-to-all-start.4 = ((bf16[16,128,128]{2,1,0:T(8,128)(2,1)}), bf16[16,128,128]{2,1,0:T(8,128)(2,1)}, u32[]{:S(2)}, u32[]{:S(2)}) async-start(bf16[16,128,128]{2,1,0:T(8,128)(2,1)} %bitcast.137), calls=%async_computation.4 | async-start | bytes 1048576 | tf_op jit(solution)/shard_map/all_to_all | solution.py:113
  217.2 14.0 %all-to-all-done.4 = bf16[16,128,128]{2,1,0:T(8,128)(2,1)} async-done(((bf16[16,128,128]{2,1,0:T(8,128)(2,1)}), bf16[16,128,128]{2,1,0:T(8,128)(2,1)}, u32[]{:S(2)}, u32[]{:S(2)}) %all-to-all-start.4) | async-done | bytes 524320 | tf_op jit(solution)/shard_map/all_to_all | solution.py:113
  231.2 28.0 %all_to_all.133 = bf16[16,128,128]{2,1,0:T(8,128)(2,1)S(1)} all-to-all(bf16[16,128,128]{2,1,0:T(8,128)(2,1)S(1)} %bitcast.135), channel_id=1, replica_groups=mesh['dp'=8,'pipe'=4,'seq'=16] {'seq'}, dimensions={0} | all-to-all | bytes 1048576 | tf_op jit(solution)/shard_map/all_to_all | solution.py:115
  259.3 2.4 stack.3
  261.7 6.9 %all-to-all-start.7 = ((bf16[16,256,512]{2,1,0:T(8,128)(2,1)}), bf16[16,256,512]{2,1,0:T(8,128)(2,1)}, u32[]{:S(2)}, u32[]{:S(2)}) async-start(bf16[16,256,512]{2,1,0:T(8,128)(2,1)} %stack.3), calls=%async_computation.7 | async-start | bytes 8388608 | tf_op jit(solution)/shard_map/all_to_all | solution.py:14
  271.3 227.9 %all-gather.2.cloned.1.call-done = bf16[2048,512]{0,1:T(8,128)(2,1)} async-done(((bf16[128,512]{0,1:T(8,128)(2,1)}), bf16[2048,512]{0,1:T(8,128)(2,1)}) %all-gather.2.cloned.1.call-update) | async-done | bytes 2097168 | tf_op jit(solution)/shard_map/all_gather | solution.py:125
  499.1 3.0 fusion.22
  506.7 125.6 %all-reduce.4.cloned.1.call-done = bf16[1,256,512]{1,2,0:T(8,128)(2,1)} async-done(((bf16[1,256,512]{1,2,0:T(8,128)(2,1)}), bf16[1,256,512]{1,2,0:T(8,128)(2,1)}) %all-reduce.4.cloned.1.call-update) | async-done | bytes 262160 | tf_op jit(solution)/shard_map/psum | solution.py:129
  634.2 4.7 fusion
  (171 shorter events, 54.0 us)
Async XLA Ops:
  7.2 19.8 %copy-start.34 = (bf16[1,1,128,2048]{3,2,1,0:T(8,128)(2,1)S(1)}, bf16[1,1,128,2048]{3,2,1,0:T(8,128)(2,1)}, u32[]{:S(2)}) copy-start(bf16[1,1,128,2048]{3,2,1,0:T(8,128)(2,1)} %param.26) | copy-start | bytes 1572868
  8.2 44.9 %copy-start.42 = (bf16[1,1,128,512]{3,2,1,0:T(8,128)(2,1)S(1)}, bf16[1,1,128,512]{3,2,1,0:T(8,128)(2,1)}, u32[]{:S(2)}) copy-start(bf16[1,1,128,512]{3,2,1,0:T(8,128)(2,1)} %param.28) | copy-start | bytes 393220
  8.2 44.9 %copy-start.26 = (bf16[1,1,128,4096]{3,2,1,0:T(8,128)(2,1)S(1)}, bf16[1,1,128,4096]{3,2,1,0:T(8,128)(2,1)}, u32[]{:S(2)}) copy-start(bf16[1,1,128,4096]{3,2,1,0:T(8,128)(2,1)} %param.30) | copy-start | bytes 3145732
  9.1 37.9 %all-to-all-start.1 = ((bf16[128,16,128]{2,0,1:T(8,128)(2,1)}), bf16[128,16,128]{2,0,1:T(8,128)(2,1)S(1)}, u32[]{:S(2)}, u32[]{:S(2)}) async-start(bf16[128,16,128]{2,0,1:T(8,128)(2,1)} %bitcast.3), calls=%async_computation.1 | async-start | bytes 1048576 | tf_op jit(solution)/shard_map/all_to_all | solution.py:104
  47.0 37.7 %copy-start.13 = (bf16[128,16,128]{2,0,1:T(8,128)(2,1)}, bf16[128,16,128]{2,0,1:T(8,128)(2,1)S(1)}, u32[]{:S(2)}) copy-start(bf16[128,16,128]{2,0,1:T(8,128)(2,1)S(1)} %all-to-all-done.1) | copy-start | bytes 1572868
  47.0 23.1 %all-to-all-start = ((bf16[128,16,128]{0,2,1:T(8,128)(2,1)}), bf16[128,16,128]{0,2,1:T(8,128)(2,1)S(1)}, u32[]{:S(2)}, u32[]{:S(2)}) async-start(bf16[128,16,128]{0,2,1:T(8,128)(2,1)} %bitcast), calls=%async_computation | async-start | bytes 1048576 | tf_op jit(solution)/shard_map/all_to_all | solution.py:103
  50.6 28.0 %collective-permute-start = (bf16[128,2048]{1,0:T(8,128)(2,1)}, bf16[128,2048]{1,0:T(8,128)(2,1)S(1)}, u32[]{:S(2)}, u32[]{:S(2)}) collective-permute-start(bf16[128,2048]{1,0:T(8,128)(2,1)} %bitcast.162), channel_id=1, source_target_pairs={{16,0},{32,16},{48,32},{0,48},{17,1},{33,17},{49,33},{1,49},{18,2}... | collective-permute-start | bytes 1572872 | tf_op jit(solution)/shard_map/ppermute | solution.py:21
  71.0 27.2 %all-to-all-start.3 = ((bf16[128,16,128]{2,0,1:T(8,128)(2,1)}), bf16[128,16,128]{2,0,1:T(8,128)(2,1)S(1)}, u32[]{:S(2)}, u32[]{:S(2)}) async-start(bf16[128,16,128]{2,0,1:T(8,128)(2,1)} %bitcast.9), calls=%async_computation.3 | async-start | bytes 1048576 | tf_op jit(solution)/shard_map/all_to_all | solution.py:105
  84.7 24.5 %copy-start.11 = (f32[512,512]{0,1:T(8,128)}, f32[512,512]{0,1:T(8,128)S(1)}, u32[]{:S(2)}) copy-start(f32[512,512]{0,1:T(8,128)S(1)} %get-tuple-element.151) | copy-start | bytes 3145732
  87.5 22.6 %copy-start.45 = (f32[512]{0:T(512)}, f32[512]{0:T(512)S(1)}, u32[]{:S(2)}) copy-start(f32[512]{0:T(512)S(1)} %get-tuple-element.144) | copy-start | bytes 6148
  98.2 12.0 %copy-start.7 = (bf16[128,16,128]{2,0,1:T(8,128)(2,1)}, bf16[128,16,128]{2,0,1:T(8,128)(2,1)S(1)}, u32[]{:S(2)}) copy-start(bf16[128,16,128]{2,0,1:T(8,128)(2,1)S(1)} %all-to-all-done.3) | copy-start | bytes 1572868
  98.2 29.0 %all-to-all-start.2 = ((bf16[128,16,128]{0,2,1:T(8,128)(2,1)}), bf16[128,16,128]{0,2,1:T(8,128)(2,1)}, u32[]{:S(2)}, u32[]{:S(2)}) async-start(bf16[128,16,128]{0,2,1:T(8,128)(2,1)} %bitcast.7), calls=%async_computation.2 | async-start | bytes 1048576 | tf_op jit(solution)/shard_map/all_to_all | solution.py:106
  127.2 31.5 %all-to-all-start.8 = ((bf16[128,16,256]{0,2,1:T(8,128)(2,1)}), bf16[128,16,256]{0,2,1:T(8,128)(2,1)}, u32[]{:S(2)}, u32[]{:S(2)}) async-start(bf16[128,16,256]{0,2,1:T(8,128)(2,1)} %bitcast.127), calls=%async_computation.8 | async-start | bytes 2097152 | tf_op jit(solution)/shard_map/all_to_all | solution.py:124
  134.5 12.9 %copy-start.19 = (bf16[4,16,8,128]{3,2,1,0:T(8,128)(2,1)}, bf16[4,16,8,128]{3,2,1,0:T(8,128)(2,1)S(1)}, u32[]{:S(2)}) copy-start(bf16[4,16,8,128]{3,2,1,0:T(8,128)(2,1)S(1)} %get-tuple-element.137) | copy-start | bytes 393220
  151.4 20.5 %copy-start.24 = (bf16[12,128,128]{2,1,0:T(8,128)(2,1)S(1)}, bf16[12,128,128]{2,1,0:T(8,128)(2,1)}, u32[]{:S(2)}) copy-start(bf16[12,128,128]{2,1,0:T(8,128)(2,1)} %copy-done.23) | copy-start | bytes 1179652
  158.7 45.7 %all-to-all-start.5 = ((bf16[16,128,128]{2,1,0:T(8,128)(2,1)}), bf16[16,128,128]{2,1,0:T(8,128)(2,1)}, u32[]{:S(2)}, u32[]{:S(2)}) async-start(bf16[16,128,128]{2,1,0:T(8,128)(2,1)} %bitcast.138), calls=%async_computation.5 | async-start | bytes 1048576 | tf_op jit(solution)/shard_map/all_to_all | solution.py:114
  172.5 39.1 %copy-start.37 = (bf16[4,16,8,128]{3,2,1,0:T(8,128)(2,1)S(1)}, bf16[4,16,8,128]{3,2,1,0:T(8,128)(2,1)}, u32[]{:S(2)}) copy-start(bf16[4,16,8,128]{3,2,1,0:T(8,128)(2,1)} %copy-done.36) | copy-start | bytes 393220
  173.2 40.0 %copy-start.44 = (bf16[4,16,8,128]{3,2,1,0:T(8,128)(2,1)S(1)}, bf16[4,16,8,128]{3,2,1,0:T(8,128)(2,1)}, u32[]{:S(2)}) copy-start(bf16[4,16,8,128]{3,2,1,0:T(8,128)(2,1)} %copy-done.43) | copy-start | bytes 393220
  204.3 26.9 %all-to-all-start.4 = ((bf16[16,128,128]{2,1,0:T(8,128)(2,1)}), bf16[16,128,128]{2,1,0:T(8,128)(2,1)}, u32[]{:S(2)}, u32[]{:S(2)}) async-start(bf16[16,128,128]{2,1,0:T(8,128)(2,1)} %bitcast.137), calls=%async_computation.4 | async-start | bytes 1048576 | tf_op jit(solution)/shard_map/all_to_all | solution.py:113
  216.5 42.8 %copy-start.40 = (bf16[1,256,512]{2,1,0:T(8,128)(2,1)S(1)}, bf16[1,256,512]{2,1,0:T(8,128)(2,1)}, u32[]{:S(2)}) copy-start(bf16[1,256,512]{2,1,0:T(8,128)(2,1)} %param.31) | copy-start | bytes 786436
  261.7 372.5 %all-to-all-start.7 = ((bf16[16,256,512]{2,1,0:T(8,128)(2,1)}), bf16[16,256,512]{2,1,0:T(8,128)(2,1)}, u32[]{:S(2)}, u32[]{:S(2)}) async-start(bf16[16,256,512]{2,1,0:T(8,128)(2,1)} %stack.3), calls=%async_computation.7 | async-start | bytes 8388608 | tf_op jit(solution)/shard_map/all_to_all | solution.py:14
  268.6 230.6 %all-gather.2.cloned.1.call-start = ((), (), s32[]{:S(2)}) async-start(), calls=%async_computation.9 | async-start | bytes 2228224 | tf_op jit(solution)/shard_map/all_gather | solution.py:125
  269.5 362.8 %all-reduce.4.cloned.1.call-start = ((), (), s32[]{:S(2)}) async-start(), calls=%async_computation.10 | async-start | bytes 524288 | tf_op jit(solution)/shard_map/psum | solution.py:129
  502.2 132.0 %copy-start.25 = (bf16[128,4,128]{0,2,1:T(8,128)(2,1)S(1)}, bf16[128,4,128]{0,2,1:T(8,128)(2,1)}, u32[]{:S(2)}) copy-start(bf16[128,4,128]{0,2,1:T(8,128)(2,1)} %copy.65) | copy-start | bytes 393220
  (37 other events, 90.2 us)
Sparse Core Ops, SparseCore 0:
  273.1 225.9 all-gather.1
  502.6 129.6 all-reduce.3
